TPU v7x, 256 devices: a whole 4x4x8 slice. The times are simulated.
256 devices in a mesh: blk: 32 (over y, z), head: 2 (over core), clip: 4 (over x).
Axes of the slice: x: 4, y: 4, z: 8, core: 2. Of those that a mesh axis runs over, the one named last changes fastest.
Arguments:
- tokens: bfloat16 [36864, 1536], P(('clip', 'blk', 'head')), parts along dimension 0, may hold values from -6 to 6
- modulation: float32 [12, 1536], P('clip'), parts along dimension 0, may hold values from -3 to 3
- w_qkv: bfloat16 [1536, 3, 1536], P(None, None, 'head'), may hold values from -0.25 to 0.25
- w_out: bfloat16 [1536, 1536], P('head'), may hold values from -0.15625 to 0.15625
- w_cross: bfloat16 [1536, 1536], P(None, 'head'), may hold values from -0.15625 to 0.15625
- q_gain: float32 [128], replicated, may hold values from 0.5 to 6
- k_gain: float32 [128], replicated, may hold values from 0.5 to 6
- cross_gain: float32 [128], replicated, may hold values from 0.5 to 6
- scene_keys: bfloat16 [8192, 1536], P(('clip', 'blk'), 'head'), parts along dimension 0, may hold values from -40 to 40
- scene_values: bfloat16 [8192, 1536], P(('clip', 'blk'), 'head'), parts along dimension 0, may hold values from -6 to 6
Outputs:
- hidden: bfloat16 [36864, 1536], P(('clip', 'blk', 'head')), parts along dimension 0
- cross_context: bfloat16 [36864, 1536], P(('clip', 'blk'), 'head'), parts along dimension 0
There are 4 independent parts, one for each index of `clip`. A program takes and returns all parts, laid end to end along the dimension named above; an argument that names none is the same for every part. Nothing has to cross between parts.
All inputs are finite; a program needn't handle non-finite values.
Results may differ from a plain program's by a relative error of at most 0.015.
The roundings to bfloat16 on the way count: a program that leaves them out, or rounds other values in their place, can miss the bound.
Values may be sent and summed in bfloat16 or wider, within the bound.
A program may use at most 128 MiB of HBM per device.

v0:
```python
import jax
import jax.numpy as jnp
from jax import lax
from jax.sharding import PartitionSpec as P

HD = 128


def head_norm(values, gain):
    rms = jnp.mean(values * values, axis=-1, keepdims=True)
    return values * lax.rsqrt(rms + 1e-06) * gain


def attend_block(carry, queries, keys_blk, values_blk):
    best, total, accum = carry
    count = keys_blk.shape[0]
    heads_here = queries.shape[1]
    width = queries.shape[2]
    keys_three = keys_blk.reshape(count, heads_here, width)
    values_three = values_blk.reshape(count, heads_here, width).astype(jnp.float32)
    scores = jnp.einsum("rhd,nhd->hrn", queries, keys_three, preferred_element_type=jnp.float32) * (
        1.0 / width**0.5
    )
    newbest = jnp.maximum(best, jnp.max(scores, axis=-1))
    factor = jnp.exp(best - newbest)
    weights = jnp.exp(scores - newbest[..., None])
    total = total * factor + jnp.sum(weights, axis=-1)
    accum = accum * jnp.transpose(factor)[..., None] + jnp.einsum(
        "hrn,nhd->rhd", weights, values_three
    )
    return (newbest, total, accum)


def attend_keys(carry, queries, keys_rows, values_rows):
    count = keys_rows.shape[0]
    blocks = count // 1024
    keys_split = keys_rows.reshape(blocks, 1024, keys_rows.shape[1])
    values_split = values_rows.reshape(blocks, 1024, values_rows.shape[1])

    def advance(state, pair):
        return (attend_block(state, queries, pair[0], pair[1]), None)

    carry, unused = lax.scan(advance, carry, (keys_split, values_split))
    return carry


def start_state(queries):
    rows = queries.shape[0]
    heads_here = queries.shape[1]
    best = jnp.full((heads_here, rows), -1e30, jnp.float32)
    total = jnp.zeros((heads_here, rows), jnp.float32)
    accum = jnp.zeros(queries.shape, jnp.float32)
    return (best, total, accum)


def finish_state(state):
    best, total, accum = state
    result = accum / jnp.transpose(total)[..., None]
    return result.reshape(result.shape[0], result.shape[1] * result.shape[2]).astype(jnp.bfloat16)


def shards(
    tokens, modulation, w_qkv, w_out, w_cross, q_gain, k_gain, cross_gain, scene_keys, scene_values
):
    width = tokens.shape[1]
    local_width = w_qkv.shape[2]
    heads_here = local_width // HD
    rows_raw = lax.all_gather(tokens, "head", axis=0, tiled=True)
    rows_count = rows_raw.shape[0]
    xfloat = rows_raw.astype(jnp.float32)
    mean = jnp.mean(xfloat, axis=-1, keepdims=True)
    var = jnp.mean((xfloat - mean) ** 2, axis=-1, keepdims=True)
    normed = (xfloat - mean) * lax.rsqrt(var + 1e-06)
    modulated = (normed * (1.0 + modulation[1]) + modulation[0]).astype(jnp.bfloat16)
    projected = jnp.dot(
        modulated, w_qkv.reshape(width, 3 * local_width), preferred_element_type=jnp.float32
    )
    projected = projected.reshape(rows_count, 3, heads_here, HD)
    queries = head_norm(projected[:, 0], q_gain).astype(jnp.bfloat16)
    keys_flat = (
        head_norm(projected[:, 1], k_gain).astype(jnp.bfloat16).reshape(rows_count, local_width)
    )
    values_flat = projected[:, 2].astype(jnp.bfloat16).reshape(rows_count, local_width)
    pieces = (
        lax.all_gather(keys_flat, "blk", axis=0, tiled=True),
        lax.all_gather(values_flat, "blk", axis=0, tiled=True),
    )
    state = attend_keys(start_state(queries), queries, pieces[0], pieces[1])
    context = finish_state(state)
    partial_sum = jnp.dot(context, w_out, preferred_element_type=jnp.float32)
    mine = lax.psum_scatter(partial_sum, "head", scatter_dimension=0, tiled=True)
    hidden = (tokens.astype(jnp.float32) + modulation[2] * mine).astype(jnp.bfloat16)
    hidden_all = lax.all_gather(hidden, "head", axis=0, tiled=True)
    cross_proj = jnp.dot(hidden_all, w_cross, preferred_element_type=jnp.float32).reshape(
        rows_count, heads_here, HD
    )
    cross_queries = head_norm(cross_proj, cross_gain).astype(jnp.bfloat16)
    pieces = (
        lax.all_gather(scene_keys, "blk", axis=0, tiled=True),
        lax.all_gather(scene_values, "blk", axis=0, tiled=True),
    )
    scene_state = attend_keys(start_state(cross_queries), cross_queries, pieces[0], pieces[1])
    cross_context = finish_state(scene_state)
    return (hidden, cross_context)


def solution(mesh):
    return jax.shard_map(
        shards,
        mesh=mesh,
        in_specs=(
            P(("clip", "blk", "head"), None),
            P("clip", None),
            P(None, None, "head"),
            P("head", None),
            P(None, "head"),
            P(),
            P(),
            P(),
            P(("clip", "blk"), "head"),
            P(("clip", "blk"), "head"),
        ),
        out_specs=(P(("clip", "blk", "head"), None), P(("clip", "blk"), "head")),
        check_vma=False,
    )
```

profile of v0, /device:TPU:1, one launch (start us, length us, event | category | flops | bytes accessed | tf_op | source)
XLA Modules:
  0.0 700.7 jit_solution(5438818760283527297)
XLA Ops:
  7.2 5.7 all_gather.18
  13.6 10.3 %copy.64 = bf16[1536,3,768]{0,2,1:T(8,128)(2,1)} copy(bf16[1536,3,768]{2,0,1:T(8,128)(2,1)} %param.16) | data formatting | bytes 14155776 | tf_op args[2]
  23.9 5.0 fusion.37
  39.2 121.7 %all-gather.5.cloned.1.call-done = bf16[9216,768]{1,0:T(8,128)(2,1)} async-done(((bf16[288,768]{1,0:T(8,128)(2,1)}), bf16[9216,768]{1,0:T(8,128)(2,1)}) %all-gather.5.cloned.1.call-update) | async-done | bytes 14155792 | tf_op jit(solution)/shard_map/all_gather | solution.py:85
  160.9 126.9 %all-gather.7.cloned.1.call-done = bf16[9216,768]{1,0:T(8,128)(2,1)} async-done(((bf16[288,768]{1,0:T(8,128)(2,1)}), bf16[9216,768]{1,0:T(8,128)(2,1)}) %all-gather.7.cloned.1.call-update) | async-done | bytes 14155792 | tf_op jit(solution)/shard_map/all_gather | solution.py:86
  287.8 194.9 %while.30 = (s32[]{:T(128)}, f32[6,288]{1,0:T(8,128)S(1)}, f32[6,288]{1,0:T(8,128)S(1)}, f32[288,6,128]{2,0,1:T(8,128)S(1)}, bf16[9,1024,768]{2,1,0:T(8,128)(2,1...) while((s32[]{:T(128)}, f32[6,288]{1,0:T(8,128)S(1)}, ...), condition=%wide.region_7.8_spmd.clone, body=%wide.region_4.7_spmd.clone.sunk | while | flops 919029888 | bytes 67596424 | solution.py:43
  287.8 3.7 constant_dynamic-slice_fusion.6
  294.2 5.5 bitcast_reduce_fusion.4
  299.6 2.6 copy.105
  302.3 4.7 fusion.88
  309.5 3.7 constant_dynamic-slice_fusion.6
  315.8 5.5 bitcast_reduce_fusion.4
  321.3 2.6 copy.105
  323.9 4.7 fusion.88
  331.1 3.7 constant_dynamic-slice_fusion.6
  337.5 5.5 bitcast_reduce_fusion.4
  343.0 2.6 copy.105
  345.6 4.7 fusion.88
  352.8 3.7 constant_dynamic-slice_fusion.6
  359.1 5.5 bitcast_reduce_fusion.4
  367.2 4.7 fusion.88
  374.4 3.7 constant_dynamic-slice_fusion.6
  380.8 5.5 bitcast_reduce_fusion.4
  388.9 4.7 fusion.88
  396.1 3.7 constant_dynamic-slice_fusion.6
  402.4 5.5 bitcast_reduce_fusion.4
  410.5 4.7 fusion.88
  417.7 3.7 constant_dynamic-slice_fusion.6
  424.1 5.5 bitcast_reduce_fusion.4
  432.2 4.7 fusion.88
  439.4 3.7 constant_dynamic-slice_fusion.6
  445.7 5.5 bitcast_reduce_fusion.4
  451.2 2.6 copy.105
  453.8 4.7 fusion.88
  461.1 3.7 constant_dynamic-slice_fusion.6
  467.4 5.5 bitcast_reduce_fusion.4
  475.5 4.7 fusion.88
  486.1 11.6 %reduce-scatter.2.cloned.1.call-done = f32[144,1536]{1,0:T(8,128)} async-done(((f32[288,1536]{1,0:T(8,128)}), f32[144,1536]{1,0:T(8,128)}) %reduce-scatter.2.cloned.1.call-update) | async-done | bytes 884752 | tf_op jit(solution)/shard_map/reduce_scatter | solution.py:91
  499.1 2.6 all_gather.22
  505.5 71.6 %all-gather.9.cloned.1.call-done = bf16[2048,768]{1,0:T(8,128)(2,1)} async-done(((bf16[64,768]{1,0:T(8,128)(2,1)}), bf16[2048,768]{1,0:T(8,128)(2,1)}) %all-gather.9.cloned.1.call-update) | async-done | bytes 3145744 | tf_op jit(solution)/shard_map/all_gather | solution.py:99
  577.2 79.4 %all-gather.11.cloned.1.call-done = bf16[2048,768]{1,0:T(8,128)(2,1)} async-done(((bf16[64,768]{1,0:T(8,128)(2,1)}), bf16[2048,768]{1,0:T(8,128)(2,1)}) %all-gather.11.cloned.1.call-update) | async-done | bytes 3145744 | tf_op jit(solution)/shard_map/all_gather | solution.py:100
  656.5 35.9 %while.31 = (s32[]{:T(128)}, f32[6,288]{1,0:T(8,128)S(1)}, f32[6,288]{1,0:T(8,128)S(1)}, f32[288,6,128]{2,0,1:T(8,128)S(1)}, bf16[2,1024,768]{2,1,0:T(8,128)(2,1...) while((s32[]{:T(128)}, f32[6,288]{1,0:T(8,128)S(1)}, ...), condition=%wide.region_13.14_spmd.clone, body=%wide.region_10.13_spmd.clone.sunk | while | flops 919029888 | bytes 67596424 | solution.py:43
  656.5 3.7 constant_dynamic-slice_fusion.7
  662.0 4.0 bitcast_reduce_fusion.5
  667.7 4.4 fusion.96
  674.5 3.7 constant_dynamic-slice_fusion.7
  679.9 4.0 bitcast_reduce_fusion.5
  685.6 4.4 fusion.96
  (145 shorter events, 91.4 us)
Async XLA Ops:
  7.2 475.5 %copy-start = (bf16[768,1536]{1,0:T(8,128)(2,1)S(1)}, bf16[768,1536]{1,0:T(8,128)(2,1)}, u32[]{:S(2)}) copy-start(bf16[768,1536]{1,0:T(8,128)(2,1)} %param.17) | copy-start | bytes 7077892
  7.2 6.3 copy-start.6
  7.2 153.7 %all-gather.5.cloned.1.call-start = ((), (), s32[]{:S(2)}) async-start(), calls=%async_computation.1 | async-start | bytes 14598144 | tf_op jit(solution)/shard_map/all_gather | solution.py:85
  28.9 1.6 copy-start.4
  30.5 1.1 copy-start.9
  33.0 4.0 copy-start.7
  33.0 254.8 %all-gather.7.cloned.1.call-start = ((), (), s32[]{:S(2)}) async-start(), calls=%async_computation.2 | async-start | bytes 14598144 | tf_op jit(solution)/shard_map/all_gather | solution.py:86
  35.3 462.4 %reduce-scatter.2.cloned.1.call-start = ((), (), s32[]{:S(2)}) async-start(), calls=%async_computation.3 | async-start | bytes 2654208 | tf_op jit(solution)/shard_map/reduce_scatter | solution.py:91
  302.3 5.5 copy-start.2
  323.9 5.5 copy-start.2
  345.6 5.5 copy-start.2
  367.2 5.5 copy-start.2
  388.9 5.5 copy-start.2
  410.5 5.5 copy-start.2
  432.2 5.5 copy-start.2
  453.8 5.5 copy-start.2
  475.5 5.5 copy-start.2
  484.9 92.3 %all-gather.9.cloned.1.call-start = ((), (), s32[]{:S(2)}) async-start(), calls=%async_computation.4 | async-start | bytes 3244032 | tf_op jit(solution)/shard_map/all_gather | solution.py:99
  485.4 171.1 %all-gather.11.cloned.1.call-start = ((), (), s32[]{:S(2)}) async-start(), calls=%async_computation.5 | async-start | bytes 3244032 | tf_op jit(solution)/shard_map/all_gather | solution.py:100
  499.1 2.6 copy-start.5
  504.3 0.8 copy-start.8
  667.7 5.1 copy-start.3
  685.6 5.1 copy-start.3
  692.4 1.8 copy-start.1
Sparse Core Ops, SparseCore 0:
  33.1 127.7 all-gather.4
  163.5 124.2 all-gather.6
  485.0 12.6 reduce-scatter.1
  500.5 76.6 all-gather.8
  579.9 76.5 all-gather.10
where the time goes:
time: 705 us; the launch traced here: 701 us
  waiting for transfers between devices  412 us (58%)
  local copies, waits for them, and re-layouts  120 us (17%)
  matrix products  118 us (17%)
  other arithmetic  27.2 us (4%)
  between operations  14.1 us (2%)
  blocking collectives  8.27 us (1%)
    all_gather x1, waiting for transfers between devices, shards(): lax.all_gather(values_flat, 'blk', axis=0, tiled=True)  127 us
    all_gather x1, waiting for transfers between devices, shards(): lax.all_gather(keys_flat, 'blk', axis=0, tiled=True)  122 us
    dynamic_slice x33, local copies, waits for them, and re-layouts, attend_keys(): carry, unused = lax.scan(advance, carry, (keys_split, values_split))  94.9 us
    all_gather x1, waiting for transfers between devices, shards(): lax.all_gather(scene_values, 'blk', axis=0, tiled=True)  79.4 us
    all_gather x1, waiting for transfers between devices, shards(): lax.all_gather(scene_keys, 'blk', axis=0, tiled=True)  71.6 us
    dot_general x11, matrix products, attend_block(): jnp.einsum('rhd,nhd->hrn', queries, keys_three, preferred_element_type=jn...  57.3 us
    dot_general x11, matrix products, attend_block(): jnp.einsum('hrn,nhd->rhd', weights, values_three)  51.1 us
    reduce_sum x11, other arithmetic, attend_block(): total = total * factor + jnp.sum(weights, axis=-1)  17.8 us
  transfers between devices with their start and end apart: 5, of which 5 were waited for; matrix products, arithmetic and copies ran while one was open for 2% of the time, Pallas kernels for 0%

commit v1 on v0

v1 whole, which is shorter than its diff:
```python
import functools

import jax
import jax.numpy as jnp
from jax import lax
from jax.experimental import pallas as pl
from jax.experimental.pallas import tpu as pltpu
from jax.sharding import PartitionSpec as P

HD = 128
NY, NZ = 4, 8
F32, BF16 = jnp.float32, jnp.bfloat16
MESH = pl.DeviceIdType.MESH
SCALE2 = 1.4426950408889634 / HD**0.5
SAFE_EXPONENT = 96.0
MAIN = (0, 2, 3, 5)
SHARED = (1, 1, 4, 4)
ORDER = ((1, 7), (0, 4), (2, 6), (3, 5))


def head_norm(values, gain):
    rms = jnp.mean(values * values, axis=-1, keepdims=True)
    return values * lax.rsqrt(rms + 1e-06) * gain


def device(y, z, core):
    return {"blk": y * NZ + z, "head": core}


def source_core(z):
    return lax.rem(z // 2, 2)


def main_of(z):
    return 3 * (z // 4) + 2 * lax.rem(z, 2)


def shared_of(z):
    return 3 * (z // 4) + 1


def put(src, dst, send_sem, recv_sem, target, same):
    @pl.when(same)
    def _():
        pltpu.make_async_copy(src, dst, recv_sem).start()

    @pl.when(jnp.logical_not(same))
    def _():
        pltpu.make_async_remote_copy(src, dst, send_sem, recv_sem, target, MESH).start()


def landed(dst, recv_sem):
    pltpu.make_async_copy(dst, dst, recv_sem).wait()


def sent(src, send_sem, same):
    @pl.when(jnp.logical_not(same))
    def _():
        landed(src, send_sem)


def greet(y, z, core):
    barrier = pltpu.get_barrier_semaphore()
    for d in range(NZ):
        for e in range(2):
            if d or e:
                to = device(y, lax.rem(z + d, NZ), lax.rem(core + e, 2))
                pl.semaphore_signal(barrier, inc=1, device_id=to, device_id_type=MESH)
    for d in range(1, NY):
        to = device(lax.rem(y + d, NY), z, core)
        pl.semaphore_signal(barrier, inc=1, device_id=to, device_id_type=MESH)
    pl.semaphore_wait(barrier, 2 * NZ - 1 + NY - 1)


def scores_of(q, k):
    return lax.dot_general(q, k, (((1,), (1,)), ((), ())), preferred_element_type=F32)


def attend(use_max, q, k, v, acc, best, rows):
    s = scores_of(q, k)
    wide = jnp.concatenate([v, jnp.ones_like(v)], axis=1)
    if use_max:
        s = s * SCALE2
        old = best[rows, :]
        new = jnp.maximum(old, jnp.max(s, axis=1, keepdims=True))
        best[rows, :] = new
        p = jnp.exp2(s - new[:, :1]).astype(BF16)
        factor = jnp.exp2(old - new)
        kept = acc[rows, :] * jnp.concatenate([factor, factor], axis=1)
        acc[rows, :] = kept + jnp.dot(p, wide, preferred_element_type=F32)
    else:
        p = jnp.exp2(s * SCALE2).astype(BF16)
        acc[rows, :] += jnp.dot(p, wide, preferred_element_type=F32)


def block_kernel(
    use_max, half, sc_half,
    tok_ref, mod_ref, w_ref, wo_ref, wc_ref, qg_ref, kg_ref, cg_ref, sk_ref, sv_ref,
    hid_ref, out_ref,
    w, wo, wc, mod, kv_out, qm, qs, sc_out, kv, qbuf, acc, best, ctx, ctx_in, scene, hid, cqm, cqs, cqbuf,
    s_w, s_x, r_x, s_z, s_s, s_q, s_cq, s_yp, s_ym, s_co, s_sy, s_sc, s_c, s_cc,
    r_kv, r_co, r_s, r_sy, r_sc, r_q, r_cq, r_c, r_cc,
):
    blk = lax.axis_index("blk")
    y, z, core = blk // NZ, lax.rem(blk, NZ), lax.axis_index("head")
    other = 1 - core
    block = NY * 2 * half
    count = 4 * half
    deep = wo_ref.shape[0]
    up, down, far = lax.rem(y + 1, NY), lax.rem(y + NY - 1, NY), lax.rem(y + 2, NY)
    mine = pl.ds(pl.multiple_of(core * half, 16), half)
    theirs = pl.ds(pl.multiple_of(other * half, 16), half)
    my_rows = pl.ds(pl.multiple_of(core * deep, 16), deep)
    their_rows = pl.ds(pl.multiple_of(other * deep, 16), deep)

    for at, p in enumerate((1, 2, 0)):
        pltpu.make_async_copy(w_ref.at[p], w.at[p], s_w.at[p]).start()
    pltpu.make_async_copy(wo_ref, wo.at[my_rows, :], s_w.at[3]).start()
    pltpu.make_async_copy(wc_ref, wc, s_w.at[4]).start()
    x = tok_ref[...].astype(F32)
    mean = jnp.mean(x, axis=-1, keepdims=True)
    var = jnp.mean((x - mean) ** 2, axis=-1, keepdims=True)
    normed = (x - mean) * lax.rsqrt(var + 1e-06)
    mod[mine, :] = (normed * (1.0 + mod_ref[1:2, :]) + mod_ref[0:1, :]).astype(BF16)
    greet(y, z, core)
    sibling = device(y, z, other)

    def to_sibling(src, dst, i):
        return pltpu.make_async_remote_copy(src, dst, s_x.at[i], r_x.at[i], sibling, MESH)

    to_sibling(mod.at[mine, :], mod.at[mine, :], 0).start()
    landed(mod.at[theirs, :], r_x.at[0])
    to_sibling(wo_ref, wo.at[my_rows, :], 1).start()

    def project(left, weights, i):
        return jnp.dot(left[...], weights[:, 256 * i : 256 * i + 256], preferred_element_type=F32)

    for i in range(3):
        for at, h in ((0, 2 * i), (128, 2 * i + 1)):
            cols = slice(h * HD, (h + 1) * HD)
            for j in range(4):
                if MAIN[j] == h:
                    sc_out[j, :, 0:128] = sk_ref[:, cols]
                    sc_out[j, :, 256:384] = sv_ref[:, cols]
                if SHARED[j] == h:
                    sc_out[j, :, 128:256] = sk_ref[:, cols]
                    sc_out[j, :, 384:512] = sv_ref[:, cols]
    for p in (1, 2):
        landed(w.at[p], s_w.at[p])
        for i in range(3):
            whole = project(mod, w.at[p], i)
            for at, h in ((0, 2 * i), (128, 2 * i + 1)):
                part = whole[:, at : at + 128]
                part = (head_norm(part, kg_ref[...]) if p == 1 else part).astype(BF16)
                for j in range(4):
                    if MAIN[j] == h:
                        kv_out[j, :, (p - 1) * 256 : (p - 1) * 256 + 128] = part
                    if SHARED[j] == h:
                        kv_out[j, :, (p - 1) * 256 + 128 : (p - 1) * 256 + 256] = part

    def kv_part(slot, of_y, u):
        start = slot * block + of_y * 2 * half + u * half
        return kv.at[pl.ds(pl.multiple_of(start, 16), half), :]

    def each_target(order, body):
        for d in order:
            to_z = lax.rem(z + NZ - d, NZ)

            @pl.when(source_core(to_z) == core)
            def _():
                for u in range(2):
                    same = jnp.logical_and(to_z == z, core == u)
                    body(d, to_z, 2 * (to_z // 4) + lax.rem(to_z, 2), u, device(y, to_z, u), same)

    def send_kv(c):
        def one(d, to_z, j, u, to, same):
            slot = 2 * c + ORDER[c].index(d)
            put(kv_out.at[j, pl.ds(u * half, half), :], kv_part(slot, y, u), s_z.at[d, u], r_kv.at[y, slot], to, same)

        each_target(ORDER[c], one)

    def kv_sent(c):
        packet = kv_out.at[0, pl.ds(0, half), :]
        each_target(ORDER[c], lambda d, to_z, j, u, to, same: sent(packet, s_z.at[d, u], same))

    every = (4, 0, 1, 7, 2, 6, 3, 5)

    def send_queries(main, shared, into, s_sem, r_sem):
        def one(d, to_z, j, u, to, same):
            rows = pl.ds(u * half, half)
            there = pl.ds(pl.multiple_of(z * half, 16), half)
            put(main.at[j, rows, :], into.at[there, :], s_sem.at[d, u, 0], r_sem.at[z], to, same)

            @pl.when(lax.rem(to_z, 2) == lax.rem(z, 2))
            def _():
                unit = NZ + z // 2
                there = pl.ds(pl.multiple_of(unit * half, 16), half)
                put(shared.at[j, rows, :], into.at[there, :], s_sem.at[d, u, 1], r_sem.at[unit], to, same)

        each_target(every, one)

    def queries_sent(s_sem):
        src = qm.at[0, pl.ds(0, half), :]

        def one(d, to_z, j, u, to, same):
            sent(src, s_sem.at[d, u, 0], same)

            @pl.when(lax.rem(to_z, 2) == lax.rem(z, 2))
            def _():
                sent(src, s_sem.at[d, u, 1], same)

        each_target(every, one)

    def send_scene(d, to_z, j, u, to, same):
        start = (u * NY + y) * NZ * sc_half + z * sc_half
        dst = scene.at[pl.ds(pl.multiple_of(start, 16), sc_half), :]
        put(sc_out.at[j, pl.ds(u * sc_half, sc_half), :], dst, s_s.at[d, u], r_s.at[z], to, same)

    def share(of_y, slot):
        ref = kv_part(slot, of_y, core)
        pltpu.make_async_remote_copy(ref, ref, s_co.at[of_y, slot], r_co.at[of_y, slot], sibling, MESH).start()

    def pass_on(of_y, slot, to_y, sem):
        ref = kv_part(slot, of_y, core)
        pltpu.make_async_remote_copy(ref, ref, sem, r_kv.at[of_y, slot], device(to_y, z, core), MESH).start()

    def own(c):
        for s in range(2):
            slot = 2 * c + s
            landed(kv_part(slot, y, core), r_kv.at[y, slot])
            pass_on(y, slot, up, s_yp.at[0, slot])
            pass_on(y, slot, down, s_ym.at[0, slot])
            share(y, slot)

    def near(c):
        for s in range(2):
            slot = 2 * c + s
            landed(kv_part(slot, down, core), r_kv.at[down, slot])
            if s == 0:
                pass_on(down, slot, up, s_yp.at[1, slot])
            share(down, slot)
            landed(kv_part(slot, up, core), r_kv.at[up, slot])
            if s == 1:
                pass_on(up, slot, down, s_ym.at[1, slot])
            share(up, slot)

    def farther(c):
        for s in range(2):
            slot = 2 * c + s
            landed(kv_part(slot, far, core), r_kv.at[far, slot])
            share(far, slot)

    def together(c):
        for of_y in range(NY):
            for s in range(2):
                landed(kv_part(2 * c + s, of_y, other), r_co.at[of_y, 2 * c + s])

    def scene_part(u, of_y):
        start = (u * NY + of_y) * NZ * sc_half
        return scene.at[pl.ds(pl.multiple_of(start, 16), NZ * sc_half), :]

    def share_scene(of_y):
        ref = scene_part(core, of_y)
        pltpu.make_async_remote_copy(ref, ref, s_sc.at[of_y], r_sc.at[of_y], sibling, MESH).start()

    send_kv(0)
    send_kv(1)
    landed(w.at[0], s_w.at[0])
    for i in range(3):
        whole = project(mod, w.at[0], i)
        for at, h in ((0, 2 * i), (128, 2 * i + 1)):
            part = head_norm(whole[:, at : at + 128], qg_ref[...]).astype(BF16)
            for j in range(4):
                if MAIN[j] == h:
                    qm[j, :, :] = part
                if SHARED[j] == h:
                    qs[j, :, :] = part
    acc[...] = jnp.zeros_like(acc)
    if use_max:
        best[...] = jnp.full_like(best, -1e30)
    kv_sent(0)
    send_queries(qm, qs, qbuf, s_q, r_q)
    own(0)
    kv_sent(1)
    send_kv(2)
    own(1)
    near(0)
    queries_sent(s_q)
    send_kv(3)
    each_target(every, send_scene)
    farther(0)
    for i in range(12):
        landed(qbuf.at[pl.ds(i * half, half), :], r_q.at[i])

    def step(t, unused):
        c, i = t // 3, lax.rem(t, 3)

        @pl.when(i == 0)
        def _():
            together(c)

        rows = pl.ds(pl.multiple_of(i * count, 16), count)
        keys = pl.ds(pl.multiple_of(c * 2 * block, 16), 2 * block)
        at = (i // 2) * HD
        k_cols = pl.ds(pl.multiple_of(at, HD), HD)
        v_cols = pl.ds(pl.multiple_of(at + 2 * HD, HD), HD)
        attend(use_max, qbuf[rows, :], kv[keys, k_cols], kv[keys, v_cols], acc, best, rows)

        @pl.when(jnp.logical_and(i == 0, c < 3))
        def _():
            near(c + 1)

        @pl.when(jnp.logical_and(i == 1, c < 2))
        def _():
            own(c + 2)

        @pl.when(jnp.logical_and(i == 2, c < 3))
        def _():
            farther(c + 1)

        @pl.when(t == 7)
        def _():
            for k in range(NZ):
                landed(scene.at[pl.ds(0, sc_half), :], r_s.at[k])
            ref = scene_part(core, y)
            for d in range(1, NY):
                to = device(lax.rem(y + d, NY), z, core)
                pltpu.make_async_remote_copy(ref, ref, s_sy.at[d - 1], r_sy.at[y], to, MESH).start()
            share_scene(y)

        return unused

    lax.fori_loop(0, 12, step, 0)

    def each_context(body):
        for i in range(12):
            if i < NZ:
                to_z, head = lax.rem(z + i, NZ), main_of(z)
                row = to_z * half
            else:
                to_z, head = lax.rem(z, 2) + 2 * (i - NZ), shared_of(z)
                row = i * half
            body(i, ctx.at[pl.ds(pl.multiple_of(row, 16), half), :], to_z, head)

    def send_context(i, src, to_z, head):
        head = 6 * source_core(z) + head
        cols = pl.ds(pl.multiple_of(head * HD, HD), HD)
        put(src, ctx_in.at[:, cols], s_c.at[i], r_c.at[head], device(y, to_z, core), to_z == z)

    def send_cross(i, src, to_z, head):
        cols = pl.ds(pl.multiple_of(head * HD, HD), HD)
        to_core = source_core(z)
        same = jnp.logical_and(to_z == z, to_core == core)
        put(src, out_ref.at[mine, cols], s_cc.at[i], r_cc.at[head, core], device(y, to_z, to_core), same)

    for i in range(3):
        rows = pl.ds(i * count, count)
        ctx[rows, :] = (acc[rows, 0:128] / acc[rows, 128:256]).astype(BF16)
    each_context(send_context)
    for d in range(1, NY):
        of_y = lax.rem(y + d, NY)
        landed(scene_part(core, of_y), r_sy.at[of_y])
        share_scene(of_y)
    landed(wo.at[my_rows, :], s_w.at[3])
    landed(wc, s_w.at[4])
    landed(wo.at[their_rows, :], r_x.at[1])
    for head in range(12):
        landed(ctx_in.at[:, head * HD : (head + 1) * HD], r_c.at[head])
    for i in range(wo.shape[1] // 256):
        cols = slice(256 * i, 256 * i + 256)
        new = tok_ref[:, cols].astype(F32) + mod_ref[2:3, cols] * project(ctx_in, wo, i)
        hid_ref[:, cols] = new.astype(BF16)
        hid[mine, cols] = new.astype(BF16)
    to_sibling(hid.at[mine, :], hid.at[mine, :], 2).start()
    landed(hid.at[theirs, :], r_x.at[2])
    for i in range(3):
        whole = project(hid, wc, i)
        for at, h in ((0, 2 * i), (128, 2 * i + 1)):
            part = head_norm(whole[:, at : at + 128], cg_ref[...]).astype(BF16)
            for j in range(4):
                if MAIN[j] == h:
                    cqm[j, :, :] = part
                if SHARED[j] == h:
                    cqs[j, :, :] = part
    send_queries(cqm, cqs, cqbuf, s_cq, r_cq)
    small = sc_out.at[0, pl.ds(0, sc_half), :]
    kv_sent(2)
    kv_sent(3)
    each_target(every, lambda d, to_z, j, u, to, same: sent(small, s_s.at[d, u], same))
    each_context(lambda i, src, to_z, head: sent(ctx.at[pl.ds(0, half), :], s_c.at[i], to_z == z))
    packet = kv_out.at[0, pl.ds(0, half), :]
    for slot in range(8):
        landed(packet, s_yp.at[0, slot])
        landed(packet, s_ym.at[0, slot])
        landed(packet, s_yp.at[1, slot] if slot % 2 == 0 else s_ym.at[1, slot])
        for of_y in range(NY):
            landed(packet, s_co.at[of_y, slot])
    for i in range(NY):
        landed(scene_part(other, i), r_sc.at[i])
        landed(scene_part(0, 0), s_sc.at[i])
        if i < 3:
            landed(scene_part(0, 0), s_sy.at[i])
    landed(mod.at[mine, :], s_x.at[0])
    landed(wo_ref, s_x.at[1])
    landed(hid.at[mine, :], s_x.at[2])
    for i in range(12):
        landed(cqbuf.at[pl.ds(i * half, half), :], r_cq.at[i])

    def cross_step(i, unused):
        rows = pl.ds(pl.multiple_of(i * count, 16), count)
        at = (i // 2) * HD
        k_cols = pl.ds(pl.multiple_of(at, HD), HD)
        v_cols = pl.ds(pl.multiple_of(at + 2 * HD, HD), HD)
        s = scores_of(cqbuf[rows, :], scene[:, k_cols])
        p = jnp.exp2((s - jnp.max(s, axis=1, keepdims=True)) * SCALE2).astype(BF16)
        values = scene[:, v_cols]
        wide = jnp.concatenate([values, jnp.ones_like(values)], axis=1)
        total = jnp.dot(p, wide, preferred_element_type=F32)
        ctx[rows, :] = (total[:, 0:128] / total[:, 128:256]).astype(BF16)
        return unused

    lax.fori_loop(0, 3, cross_step, 0)
    each_context(send_cross)
    for head in range(6):
        for u in range(2):
            landed(out_ref.at[pl.ds(u * half, half), head * HD : (head + 1) * HD], r_cc.at[head, u])
    queries_sent(s_cq)

    def cross_sent(i, src, to_z, head):
        same = jnp.logical_and(to_z == z, source_core(z) == core)
        sent(ctx.at[pl.ds(0, half), :], s_cc.at[i], same)

    each_context(cross_sent)


def whole_block(use_max, tokens, modulation, w_parts, w_out, w_cross, q_gain, k_gain, c_gain, sk, sv):
    half, width = tokens.shape
    sc_half = sk.shape[0] // 2
    dma = pltpu.SemaphoreType.DMA
    vmem, anywhere = pl.BlockSpec(memory_space=pltpu.VMEM), pl.BlockSpec(memory_space=pl.ANY)
    sizes = [
        (w_parts.shape, BF16), ((2 * w_out.shape[0], width), BF16), (w_cross.shape, BF16), ((2 * half, width), BF16),
        ((4, 2 * half, 4 * HD), BF16), ((4, 2 * half, HD), BF16), ((4, 2 * half, HD), BF16),
        ((4, 2 * sc_half, 4 * HD), BF16),
        ((NY * NZ * 2 * half, 4 * HD), BF16), ((12 * half, HD), BF16),
        ((12 * half, 2 * HD), F32), ((12 * half, HD), F32), ((12 * half, HD), BF16), ((half, width), BF16),
        ((2 * sc_half * NY * NZ, 4 * HD), BF16), ((2 * half, width), BF16),
        ((4, 2 * half, HD), BF16), ((4, 2 * half, HD), BF16), ((12 * half, HD), BF16),
    ]
    sems = [
        (5,), (3,), (3,), (8, 2), (8, 2), (8, 2, 2), (8, 2, 2), (2, 8), (2, 8), (4, 8), (3,), (4,), (12,), (12,),
        (4, 8), (4, 8), (8,), (4,), (4,), (12,), (12,), (12,), (6, 2),
    ]
    return pl.pallas_call(
        functools.partial(block_kernel, use_max, half, sc_half),
        out_shape=(
            jax.ShapeDtypeStruct((half, width), BF16),
            jax.ShapeDtypeStruct((2 * half, 6 * HD), BF16),
        ),
        in_specs=[vmem, vmem, anywhere, anywhere, anywhere, vmem, vmem, vmem, vmem, vmem],
        out_specs=(vmem, vmem),
        scratch_shapes=[pltpu.VMEM(s, t) for s, t in sizes] + [dma(s) for s in sems],
        compiler_params=pltpu.CompilerParams(
            collective_id=1 if use_max else 0, has_side_effects=True, vmem_limit_bytes=60 * 2**20
        ),
    )(tokens, modulation, w_parts, w_out, w_cross, q_gain, k_gain, c_gain, sk, sv)


def shards(
    tokens, modulation, w_qkv, w_out, w_cross, q_gain, k_gain, cross_gain, scene_keys, scene_values
):
    top = 1.02 * HD * SCALE2 * jnp.max(jnp.abs(q_gain)) * jnp.max(jnp.abs(k_gain))
    return lax.cond(
        top < SAFE_EXPONENT,
        functools.partial(whole_block, False),
        functools.partial(whole_block, True),
        tokens, modulation, jnp.transpose(w_qkv, (1, 0, 2)), w_out, w_cross,
        q_gain[None], k_gain[None], cross_gain[None], scene_keys, scene_values,
    )


def solution(mesh):
    return jax.shard_map(
        shards,
        mesh=mesh,
        in_specs=(
            P(("clip", "blk", "head"), None),
            P("clip", None),
            P(None, None, "head"),
            P("head", None),
            P(None, "head"),
            P(),
            P(),
            P(),
            P(("clip", "blk"), "head"),
            P(("clip", "blk"), "head"),
        ),
        out_specs=(P(("clip", "blk", "head"), None), P(("clip", "blk"), "head")),
        check_vma=False,
    )
```

time: 705 us -> 151 us (0.21)
  waiting for transfers between devices: 412 us -> 0 us
  Pallas kernels: 0 us -> 143 us
  local copies, waits for them, and re-layouts: 120 us -> 1.53 us
  matrix products: 118 us -> 0 us
  other arithmetic: 27.2 us -> 2.52 us
  between operations: 14.1 us -> 1.94 us
  blocking collectives: 8.27 us -> 0 us
    all_gather x4 -> x0, waiting for transfers between devices: 400 us -> none  [the longest x1 127 us: shards(): lax.all_gather(values_flat, 'blk', axis=0, tiled=True)]
    pallas_call x0 -> x1, Pallas kernels: none -> 143 us  [whole_block(): pl.pallas_call(functools.partial(block_kernel, use_max, half, sc_half), o...]
    dot_general x25 -> x0, matrix products: 118 us -> none  [the longest x11 57.3 us: attend_block(): jnp.einsum('rhd,nhd->hrn', queries, keys_three, preferred_element_type=jn...]
    dynamic_slice x33 -> x0, local copies, waits for them, and re-layouts: 94.9 us -> none  [attend_keys(): carry, unused = lax.scan(advance, carry, (keys_split, values_split))]
    reduce_sum x15 -> x0, other arithmetic: 20.4 us -> none  [the longest x11 17.8 us: attend_block(): total = total * factor + jnp.sum(weights, axis=-1)]
    unnamed x19 -> x2, local copies, waits for them, and re-layouts: 13.6 us -> 1.53 us
    reduce_scatter x1 -> x0, waiting for transfers between devices: 11.6 us -> none  [shards(): lax.psum_scatter(partial_sum, 'head', scatter_dimension=0, tiled=True)]
    while x33 -> x0, local copies, waits for them, and re-layouts: 8.87 us -> none
  transfers between devices with their start and end apart: 5 -> 0, of which waited for: 5 -> 0; matrix products, arithmetic and copies ran while one was open for 2% -> 0% of each run, Pallas kernels for 0% -> 0%
where the time goes in v1:
time: 151 us; the launch traced here: 149 us
  Pallas kernels  143 us (95%)
  other arithmetic  2.52 us (2%)
  between operations  1.94 us (1%)
  local copies, waits for them, and re-layouts  1.53 us (1%)
    pallas_call x1, Pallas kernels, whole_block(): pl.pallas_call(functools.partial(block_kernel, use_max, half, sc_half), o...  143 us

profile of v1, /device:TPU:1, one launch (start us, length us, event | category | flops | bytes accessed | tf_op | source)
XLA Modules:
  0.0 149.2 jit_solution(2189850668171849262)
XLA Ops:
  0.6 1.3 abs_reduce_fusion
  1.9 1.3 abs_reduce_fusion.1
  4.5 143.2 %conditional.1 = ((bf16[144,1536]{1,0:T(8,128)(2,1)S(1)}, bf16[288,768]{1,0:T(8,128)(2,1)S(1)})) conditional(s32[]{:T(128)} %convert_element_type.3, (bf16[144,1536]{1,0:T(8,128)(2,1)}, f32[3,1536]{1,0:T(4,128)}, bf16[3,1536,768]{2,1,0:T(8,128)(2,1)}, bf16[768,1536]{1,0:T(8,128)(2,1)}, bf16[1536,768]{1,0:T(8,128)(2,1)}, /*index=5*/f32[128]{0:T(128)}, ...), branch_computations={%region_2.0_spmd, %region_3.0_spmd} | conditional | bytes 8 | solution.py:473
  4.5 142.9 %branch_0_fun.1 = (bf16[144,1536]{1,0:T(8,128)(2,1)S(1)}, bf16[288,768]{1,0:T(8,128)(2,1)S(1)}) custom-call(bf16[144,1536]{1,0:T(8,128)(2,1)} %get-tuple-element.86.tok_ref, f32[3,1536]{1,0:T(4,128)} %get-tuple-element.88.mod_ref, bf16[3,1536,768]{2,1,0:T(8,128)(2,1)} %get-tuple-element.42.w_ref, bf16[768,1536]{1,0:T(8,128)(2,1)} %get-tuple-element.90.wo_ref, ...), custom_call_target="tpu_custom_call" | custom-call | tf_op jit(solution)/shard_map/cond/branch_0_fun/pallas_call | solution.py:454
  147.6 0.8 copy.36
  148.4 0.8 copy.37

commit v2 on v1

--- a/solution.py
+++ b/solution.py
@@ -16,6 +16,7 @@
 MAIN = (0, 2, 3, 5)
 SHARED = (1, 1, 4, 4)
 ORDER = ((1, 7), (0, 4), (2, 6), (3, 5))
+NEAREST = (0, 4, 1, 7, 2, 6, 3, 5)
 
 
 def head_norm(values, gain):
@@ -69,7 +70,6 @@
     for d in range(1, NY):
         to = device(lax.rem(y + d, NY), z, core)
         pl.semaphore_signal(barrier, inc=1, device_id=to, device_id_type=MESH)
-    pl.semaphore_wait(barrier, 2 * NZ - 1 + NY - 1)
 
 
 def scores_of(q, k):
@@ -113,7 +113,8 @@
     my_rows = pl.ds(pl.multiple_of(core * deep, 16), deep)
     their_rows = pl.ds(pl.multiple_of(other * deep, 16), deep)
 
-    for at, p in enumerate((1, 2, 0)):
+    greet(y, z, core)
+    for p in (1, 2, 0):
         pltpu.make_async_copy(w_ref.at[p], w.at[p], s_w.at[p]).start()
     pltpu.make_async_copy(wo_ref, wo.at[my_rows, :], s_w.at[3]).start()
     pltpu.make_async_copy(wc_ref, wc, s_w.at[4]).start()
@@ -122,7 +123,7 @@
     var = jnp.mean((x - mean) ** 2, axis=-1, keepdims=True)
     normed = (x - mean) * lax.rsqrt(var + 1e-06)
     mod[mine, :] = (normed * (1.0 + mod_ref[1:2, :]) + mod_ref[0:1, :]).astype(BF16)
-    greet(y, z, core)
+    pl.semaphore_wait(pltpu.get_barrier_semaphore(), 2 * NZ - 1 + NY - 1)
     sibling = device(y, z, other)
 
     def to_sibling(src, dst, i):
@@ -183,33 +184,24 @@
         packet = kv_out.at[0, pl.ds(0, half), :]
         each_target(ORDER[c], lambda d, to_z, j, u, to, same: sent(packet, s_z.at[d, u], same))
 
-    every = (4, 0, 1, 7, 2, 6, 3, 5)
-
     def send_queries(main, shared, into, s_sem, r_sem):
         def one(d, to_z, j, u, to, same):
-            rows = pl.ds(u * half, half)
-            there = pl.ds(pl.multiple_of(z * half, 16), half)
-            put(main.at[j, rows, :], into.at[there, :], s_sem.at[d, u, 0], r_sem.at[z], to, same)
-
-            @pl.when(lax.rem(to_z, 2) == lax.rem(z, 2))
-            def _():
-                unit = NZ + z // 2
-                there = pl.ds(pl.multiple_of(unit * half, 16), half)
-                put(shared.at[j, rows, :], into.at[there, :], s_sem.at[d, u, 1], r_sem.at[unit], to, same)
-
-        each_target(every, one)
+            unit = NEAREST.index(d)
+            there = pl.ds(unit * half, half)
+            put(main.at[j, pl.ds(u * half, half), :], into.at[there, :], s_sem.at[d, u, 0], r_sem.at[unit], to, same)
+
+        def one_shared(d, to_z, j, u, to, same):
+            unit = NZ + z // 2
+            there = pl.ds(pl.multiple_of(unit * half, 16), half)
+            put(shared.at[j, pl.ds(u * half, half), :], into.at[there, :], s_sem.at[d, u, 1], r_sem.at[unit], to, same)
+
+        each_target(NEAREST, one)
+        each_target((0, 4, 2, 6), one_shared)
 
     def queries_sent(s_sem):
         src = qm.at[0, pl.ds(0, half), :]
-
-        def one(d, to_z, j, u, to, same):
-            sent(src, s_sem.at[d, u, 0], same)
-
-            @pl.when(lax.rem(to_z, 2) == lax.rem(z, 2))
-            def _():
-                sent(src, s_sem.at[d, u, 1], same)
-
-        each_target(every, one)
+        each_target(NEAREST, lambda d, to_z, j, u, to, same: sent(src, s_sem.at[d, u, 0], same))
+        each_target((0, 4, 2, 6), lambda d, to_z, j, u, to, same: sent(src, s_sem.at[d, u, 1], same))
 
     def send_scene(d, to_z, j, u, to, same):
         start = (u * NY + y) * NZ * sc_half + z * sc_half
@@ -287,10 +279,29 @@
     near(0)
     queries_sent(s_q)
     send_kv(3)
-    each_target(every, send_scene)
+    near(1)
     farther(0)
     for i in range(12):
         landed(qbuf.at[pl.ds(i * half, half), :], r_q.at[i])
+
+    def each_context(blocks, body):
+        for i in [4 * b + k for b in blocks for k in range(4)]:
+            if i < NZ:
+                to_z, head = lax.rem(z + NEAREST[i], NZ), main_of(z)
+            else:
+                to_z, head = lax.rem(z, 2) + 2 * (i - NZ), shared_of(z)
+            body(i, ctx.at[pl.ds(i * half, half), :], to_z, head)
+
+    def send_context(i, src, to_z, head):
+        head = 6 * source_core(z) + head
+        cols = pl.ds(pl.multiple_of(head * HD, HD), HD)
+        put(src, ctx_in.at[:, cols], s_c.at[i], r_c.at[head], device(y, to_z, core), to_z == z)
+
+    def send_cross(i, src, to_z, head):
+        cols = pl.ds(pl.multiple_of(head * HD, HD), HD)
+        to_core = source_core(z)
+        same = jnp.logical_and(to_z == z, to_core == core)
+        put(src, out_ref.at[mine, cols], s_cc.at[i], r_cc.at[head, core], device(y, to_z, to_core), same)
 
     def step(t, unused):
         c, i = t // 3, lax.rem(t, 3)
@@ -306,19 +317,23 @@
         v_cols = pl.ds(pl.multiple_of(at + 2 * HD, HD), HD)
         attend(use_max, qbuf[rows, :], kv[keys, k_cols], kv[keys, v_cols], acc, best, rows)
 
-        @pl.when(jnp.logical_and(i == 0, c < 3))
-        def _():
-            near(c + 1)
-
-        @pl.when(jnp.logical_and(i == 1, c < 2))
+        @pl.when(jnp.logical_and(i == 0, c < 2))
         def _():
             own(c + 2)
 
-        @pl.when(jnp.logical_and(i == 2, c < 3))
+        @pl.when(jnp.logical_or(jnp.logical_and(i == 1, c < 2), t == 6))
         def _():
             farther(c + 1)
 
-        @pl.when(t == 7)
+        @pl.when(jnp.logical_and(i == 2, c < 2))
+        def _():
+            near(c + 2)
+
+        @pl.when(t == 3)
+        def _():
+            each_target(NEAREST, send_scene)
+
+        @pl.when(t == 6)
         def _():
             for k in range(NZ):
                 landed(scene.at[pl.ds(0, sc_half), :], r_s.at[k])
@@ -328,35 +343,17 @@
                 pltpu.make_async_remote_copy(ref, ref, s_sy.at[d - 1], r_sy.at[y], to, MESH).start()
             share_scene(y)
 
+        for last in range(3):
+
+            @pl.when(t == 9 + last)
+            def _():
+                done = pl.ds(last * count, count)
+                ctx[done, :] = (acc[done, 0:128] / acc[done, 128:256]).astype(BF16)
+                each_context((last,), send_context)
+
         return unused
 
     lax.fori_loop(0, 12, step, 0)
-
-    def each_context(body):
-        for i in range(12):
-            if i < NZ:
-                to_z, head = lax.rem(z + i, NZ), main_of(z)
-                row = to_z * half
-            else:
-                to_z, head = lax.rem(z, 2) + 2 * (i - NZ), shared_of(z)
-                row = i * half
-            body(i, ctx.at[pl.ds(pl.multiple_of(row, 16), half), :], to_z, head)
-
-    def send_context(i, src, to_z, head):
-        head = 6 * source_core(z) + head
-        cols = pl.ds(pl.multiple_of(head * HD, HD), HD)
-        put(src, ctx_in.at[:, cols], s_c.at[i], r_c.at[head], device(y, to_z, core), to_z == z)
-
-    def send_cross(i, src, to_z, head):
-        cols = pl.ds(pl.multiple_of(head * HD, HD), HD)
-        to_core = source_core(z)
-        same = jnp.logical_and(to_z == z, to_core == core)
-        put(src, out_ref.at[mine, cols], s_cc.at[i], r_cc.at[head, core], device(y, to_z, to_core), same)
-
-    for i in range(3):
-        rows = pl.ds(i * count, count)
-        ctx[rows, :] = (acc[rows, 0:128] / acc[rows, 128:256]).astype(BF16)
-    each_context(send_context)
     for d in range(1, NY):
         of_y = lax.rem(y + d, NY)
         landed(scene_part(core, of_y), r_sy.at[of_y])
@@ -386,8 +383,8 @@
     small = sc_out.at[0, pl.ds(0, sc_half), :]
     kv_sent(2)
     kv_sent(3)
-    each_target(every, lambda d, to_z, j, u, to, same: sent(small, s_s.at[d, u], same))
-    each_context(lambda i, src, to_z, head: sent(ctx.at[pl.ds(0, half), :], s_c.at[i], to_z == z))
+    each_target(NEAREST, lambda d, to_z, j, u, to, same: sent(small, s_s.at[d, u], same))
+    each_context((0, 1, 2), lambda i, src, to_z, head: sent(ctx.at[pl.ds(0, half), :], s_c.at[i], to_z == z))
     packet = kv_out.at[0, pl.ds(0, half), :]
     for slot in range(8):
         landed(packet, s_yp.at[0, slot])
@@ -403,10 +400,11 @@
     landed(mod.at[mine, :], s_x.at[0])
     landed(wo_ref, s_x.at[1])
     landed(hid.at[mine, :], s_x.at[2])
-    for i in range(12):
-        landed(cqbuf.at[pl.ds(i * half, half), :], r_cq.at[i])
 
     def cross_step(i, unused):
+        for k in range(4):
+            unit = 4 * i + k
+            landed(cqbuf.at[pl.ds(pl.multiple_of(unit * half, 16), half), :], r_cq.at[unit])
         rows = pl.ds(pl.multiple_of(i * count, 16), count)
         at = (i // 2) * HD
         k_cols = pl.ds(pl.multiple_of(at, HD), HD)
@@ -417,10 +415,15 @@
         wide = jnp.concatenate([values, jnp.ones_like(values)], axis=1)
         total = jnp.dot(p, wide, preferred_element_type=F32)
         ctx[rows, :] = (total[:, 0:128] / total[:, 128:256]).astype(BF16)
+        for last in range(3):
+
+            @pl.when(i == last)
+            def _():
+                each_context((last,), send_cross)
+
         return unused
 
     lax.fori_loop(0, 3, cross_step, 0)
-    each_context(send_cross)
     for head in range(6):
         for u in range(2):
             landed(out_ref.at[pl.ds(u * half, half), head * HD : (head + 1) * HD], r_cc.at[head, u])
@@ -430,7 +433,7 @@
         same = jnp.logical_and(to_z == z, source_core(z) == core)
         sent(ctx.at[pl.ds(0, half), :], s_cc.at[i], same)
 
-    each_context(cross_sent)
+    each_context((0, 1, 2), cross_sent)
 
 
 def whole_block(use_max, tokens, modulation, w_parts, w_out, w_cross, q_gain, k_gain, c_gain, sk, sv):
@@ -469,7 +472,7 @@
 def shards(
     tokens, modulation, w_qkv, w_out, w_cross, q_gain, k_gain, cross_gain, scene_keys, scene_values
 ):
-    top = 1.02 * HD * SCALE2 * jnp.max(jnp.abs(q_gain)) * jnp.max(jnp.abs(k_gain))
+    top = 1.02 * HD * SCALE2 * jnp.max(jnp.abs(q_gain)[:, None] * jnp.abs(k_gain)[None, :])
     return lax.cond(
         top < SAFE_EXPONENT,
         functools.partial(whole_block, False),

time: 151 us -> 132 us (0.87)
  Pallas kernels: 143 us -> 126 us
    pallas_call x1, Pallas kernels: 143 us -> 126 us  [whole_block(): pl.pallas_call(functools.partial(block_kernel, use_max, half, sc_half), o...]
    reduce_max x2 -> x1, other arithmetic: 2.52 us -> 0.69 us  [shards(): jnp.max(jnp.abs(q_gain)[:, None] * jnp.abs(k_gain)[None, :])]
where the time goes in v2:
time: 132 us
  Pallas kernels  126 us (95%)
  other arithmetic  2 us (2%)
  local copies, waits for them, and re-layouts  1.53 us (1%)
    pallas_call x1, Pallas kernels, whole_block(): pl.pallas_call(functools.partial(block_kernel, use_max, half, sc_half), o...  126 us

profile of v2, /device:TPU:1, one launch (start us, length us, event | category | flops | bytes accessed | tf_op | source)
XLA Modules:
  0.0 131.6 jit_solution(13504840249688184490)
XLA Ops:
  0.6 0.7 abs.6
  1.3 0.7 abs.7
  1.9 0.7 multiply_reduce_fusion
  3.3 126.8 %conditional.1 = ((bf16[144,1536]{1,0:T(8,128)(2,1)S(1)}, bf16[288,768]{1,0:T(8,128)(2,1)S(1)})) conditional(s32[]{:T(128)} %convert_element_type.3, (bf16[144,1536]{1,0:T(8,128)(2,1)}, f32[3,1536]{1,0:T(4,128)}, bf16[3,1536,768]{2,1,0:T(8,128)(2,1)}, bf16[768,1536]{1,0:T(8,128)(2,1)}, bf16[1536,768]{1,0:T(8,128)(2,1)}, /*index=5*/f32[128]{0:T(128)}, ...), branch_computations={%region_1.0_spmd, %region_2.0_spmd} | conditional | bytes 8 | solution.py:476
  3.3 126.3 %branch_0_fun.1 = (bf16[144,1536]{1,0:T(8,128)(2,1)S(1)}, bf16[288,768]{1,0:T(8,128)(2,1)S(1)}) custom-call(bf16[144,1536]{1,0:T(8,128)(2,1)} %get-tuple-element.86.tok_ref, f32[3,1536]{1,0:T(4,128)} %get-tuple-element.88.mod_ref, bf16[3,1536,768]{2,1,0:T(8,128)(2,1)} %get-tuple-element.42.w_ref, bf16[768,1536]{1,0:T(8,128)(2,1)} %get-tuple-element.90.wo_ref, ...), custom_call_target="tpu_custom_call" | custom-call | tf_op jit(solution)/shard_map/cond/branch_0_fun/pallas_call | solution.py:457
  130.1 0.8 copy.36
  130.9 0.8 copy.37

commit v3 on v2

--- a/solution.py
+++ b/solution.py
@@ -68,8 +68,9 @@
                 to = device(y, lax.rem(z + d, NZ), lax.rem(core + e, 2))
                 pl.semaphore_signal(barrier, inc=1, device_id=to, device_id_type=MESH)
     for d in range(1, NY):
-        to = device(lax.rem(y + d, NY), z, core)
-        pl.semaphore_signal(barrier, inc=1, device_id=to, device_id_type=MESH)
+        for e in range(2):
+            to = device(lax.rem(y + d, NY), z, lax.rem(core + e, 2))
+            pl.semaphore_signal(barrier, inc=1, device_id=to, device_id_type=MESH)
 
 
 def scores_of(q, k):
@@ -97,9 +98,9 @@
     use_max, half, sc_half,
     tok_ref, mod_ref, w_ref, wo_ref, wc_ref, qg_ref, kg_ref, cg_ref, sk_ref, sv_ref,
     hid_ref, out_ref,
-    w, wo, wc, mod, kv_out, qm, qs, sc_out, kv, qbuf, acc, best, ctx, ctx_in, scene, hid, cqm, cqs, cqbuf,
-    s_w, s_x, r_x, s_z, s_s, s_q, s_cq, s_yp, s_ym, s_co, s_sy, s_sc, s_c, s_cc,
-    r_kv, r_co, r_s, r_sy, r_sc, r_q, r_cq, r_c, r_cc,
+    w, wo, wc, mod, kv_out, qm, qs, sc_out, kv, qbuf, acc, best, ctx, ctx_in, scene, hid, cq, cqbuf,
+    s_w, s_x, r_x, s_z, s_s, s_q, s_cq, s_yp, s_ym, s_co, s_su, s_sd, s_sc, s_c, s_cc,
+    r_kv, r_co, r_s, r_sz, r_sc, r_q, r_cq, r_c, r_cc,
 ):
     blk = lax.axis_index("blk")
     y, z, core = blk // NZ, lax.rem(blk, NZ), lax.axis_index("head")
@@ -123,29 +124,67 @@
     var = jnp.mean((x - mean) ** 2, axis=-1, keepdims=True)
     normed = (x - mean) * lax.rsqrt(var + 1e-06)
     mod[mine, :] = (normed * (1.0 + mod_ref[1:2, :]) + mod_ref[0:1, :]).astype(BF16)
-    pl.semaphore_wait(pltpu.get_barrier_semaphore(), 2 * NZ - 1 + NY - 1)
+    pl.semaphore_wait(pltpu.get_barrier_semaphore(), 2 * NZ - 1 + 2 * (NY - 1))
     sibling = device(y, z, other)
 
     def to_sibling(src, dst, i):
         return pltpu.make_async_remote_copy(src, dst, s_x.at[i], r_x.at[i], sibling, MESH)
 
     to_sibling(mod.at[mine, :], mod.at[mine, :], 0).start()
+    three = 3 * HD
+    for g in range(2):
+        sc_out[g, :, 0:three] = sk_ref[:, g * three : (g + 1) * three]
+        sc_out[g, :, three : 2 * three] = sv_ref[:, g * three : (g + 1) * three]
     landed(mod.at[theirs, :], r_x.at[0])
     to_sibling(wo_ref, wo.at[my_rows, :], 1).start()
 
     def project(left, weights, i):
         return jnp.dot(left[...], weights[:, 256 * i : 256 * i + 256], preferred_element_type=F32)
 
-    for i in range(3):
-        for at, h in ((0, 2 * i), (128, 2 * i + 1)):
-            cols = slice(h * HD, (h + 1) * HD)
-            for j in range(4):
-                if MAIN[j] == h:
-                    sc_out[j, :, 0:128] = sk_ref[:, cols]
-                    sc_out[j, :, 256:384] = sv_ref[:, cols]
-                if SHARED[j] == h:
-                    sc_out[j, :, 128:256] = sk_ref[:, cols]
-                    sc_out[j, :, 384:512] = sv_ref[:, cols]
+    def each_ring(body):
+        for g in range(2):
+            for u in range(2):
+                to_y = 2 * core + g
+                body(g, u, device(to_y, z, u), jnp.logical_and(to_y == y, core == u))
+
+    def scene_part(u, of_z):
+        start = (u * NZ + of_z) * NY * sc_half
+        return scene.at[pl.ds(pl.multiple_of(start, 16), NY * sc_half), :]
+
+    def send_scene(g, u, to, same):
+        start = ((u * NZ + z) * NY + y) * sc_half
+        dst = scene.at[pl.ds(pl.multiple_of(start, 16), sc_half), :]
+        put(sc_out.at[g, pl.ds(u * sc_half, sc_half), :], dst, s_s.at[g, u], r_s.at[y], to, same)
+
+    def pass_scene(of_z, d, sem):
+        ref = scene_part(core, of_z)
+        to = device(y, lax.rem(z + NZ + d, NZ), core)
+        pltpu.make_async_remote_copy(ref, ref, sem, r_sz.at[of_z], to, MESH).start()
+
+    def share_scene(of_z):
+        ref = scene_part(core, of_z)
+        pltpu.make_async_remote_copy(ref, ref, s_sc.at[of_z], r_sc.at[of_z], sibling, MESH).start()
+
+    def ring_scene(k):
+        if k == 0:
+            for i in range(NY):
+                landed(scene.at[pl.ds(0, sc_half), :], r_s.at[i])
+            pass_scene(z, 1, s_su.at[0])
+            pass_scene(z, -1, s_sd.at[0])
+            share_scene(z)
+            return
+        below, above = lax.rem(z + NZ - k, NZ), lax.rem(z + k, NZ)
+        landed(scene_part(core, below), r_sz.at[below])
+        if k < 4:
+            pass_scene(below, 1, s_su.at[k])
+        share_scene(below)
+        if k < 4:
+            landed(scene_part(core, above), r_sz.at[above])
+            if k < 3:
+                pass_scene(above, -1, s_sd.at[k])
+            share_scene(above)
+
+    each_ring(send_scene)
     for p in (1, 2):
         landed(w.at[p], s_w.at[p])
         for i in range(3):
@@ -184,29 +223,25 @@
         packet = kv_out.at[0, pl.ds(0, half), :]
         each_target(ORDER[c], lambda d, to_z, j, u, to, same: sent(packet, s_z.at[d, u], same))
 
-    def send_queries(main, shared, into, s_sem, r_sem):
+    def send_main(order, main, into, s_sem, r_sem):
         def one(d, to_z, j, u, to, same):
             unit = NEAREST.index(d)
             there = pl.ds(unit * half, half)
             put(main.at[j, pl.ds(u * half, half), :], into.at[there, :], s_sem.at[d, u, 0], r_sem.at[unit], to, same)
 
-        def one_shared(d, to_z, j, u, to, same):
+        each_target(order, one)
+
+    def send_shared(shared, into, s_sem, r_sem):
+        def one(d, to_z, j, u, to, same):
             unit = NZ + z // 2
             there = pl.ds(pl.multiple_of(unit * half, 16), half)
             put(shared.at[j, pl.ds(u * half, half), :], into.at[there, :], s_sem.at[d, u, 1], r_sem.at[unit], to, same)
 
-        each_target(NEAREST, one)
-        each_target((0, 4, 2, 6), one_shared)
-
-    def queries_sent(s_sem):
+        each_target((0, 4, 2, 6), one)
+
+    def queries_sent(order, s_sem, which):
         src = qm.at[0, pl.ds(0, half), :]
-        each_target(NEAREST, lambda d, to_z, j, u, to, same: sent(src, s_sem.at[d, u, 0], same))
-        each_target((0, 4, 2, 6), lambda d, to_z, j, u, to, same: sent(src, s_sem.at[d, u, 1], same))
-
-    def send_scene(d, to_z, j, u, to, same):
-        start = (u * NY + y) * NZ * sc_half + z * sc_half
-        dst = scene.at[pl.ds(pl.multiple_of(start, 16), sc_half), :]
-        put(sc_out.at[j, pl.ds(u * sc_half, sc_half), :], dst, s_s.at[d, u], r_s.at[z], to, same)
+        each_target(order, lambda d, to_z, j, u, to, same: sent(src, s_sem.at[d, u, which], same))
 
     def share(of_y, slot):
         ref = kv_part(slot, of_y, core)
@@ -246,14 +281,6 @@
         for of_y in range(NY):
             for s in range(2):
                 landed(kv_part(2 * c + s, of_y, other), r_co.at[of_y, 2 * c + s])
-
-    def scene_part(u, of_y):
-        start = (u * NY + of_y) * NZ * sc_half
-        return scene.at[pl.ds(pl.multiple_of(start, 16), NZ * sc_half), :]
-
-    def share_scene(of_y):
-        ref = scene_part(core, of_y)
-        pltpu.make_async_remote_copy(ref, ref, s_sc.at[of_y], r_sc.at[of_y], sibling, MESH).start()
 
     send_kv(0)
     send_kv(1)
@@ -271,17 +298,18 @@
     if use_max:
         best[...] = jnp.full_like(best, -1e30)
     kv_sent(0)
-    send_queries(qm, qs, qbuf, s_q, r_q)
+    send_main(NEAREST, qm, qbuf, s_q, r_q)
     own(0)
     kv_sent(1)
     send_kv(2)
     own(1)
     near(0)
-    queries_sent(s_q)
+    queries_sent(NEAREST, s_q, 0)
     send_kv(3)
     near(1)
     farther(0)
-    for i in range(12):
+    ring_scene(0)
+    for i in range(NZ):
         landed(qbuf.at[pl.ds(i * half, half), :], r_q.at[i])
 
     def each_context(blocks, body):
@@ -297,51 +325,54 @@
         cols = pl.ds(pl.multiple_of(head * HD, HD), HD)
         put(src, ctx_in.at[:, cols], s_c.at[i], r_c.at[head], device(y, to_z, core), to_z == z)
 
-    def send_cross(i, src, to_z, head):
+    def each_cross(i, body):
+        for k in range(NY):
+            to_y, to_core = lax.rem(y + k, NY), y // 2
+            same = jnp.logical_and(to_y == y, to_core == core)
+            src = ctx.at[pl.ds(pl.multiple_of((i * NY + to_y) * half, 16), half), :]
+            body(src, s_cc.at[i * NY + k], device(to_y, z, to_core), same)
+
+    def send_cross(i, src, sem, to, same):
+        head = 3 * lax.rem(y, 2) + i
         cols = pl.ds(pl.multiple_of(head * HD, HD), HD)
-        to_core = source_core(z)
-        same = jnp.logical_and(to_z == z, to_core == core)
-        put(src, out_ref.at[mine, cols], s_cc.at[i], r_cc.at[head, core], device(y, to_z, to_core), same)
+        put(src, out_ref.at[mine, cols], sem, r_cc.at[head, core], to, same)
+
+    def start_shared():
+        own(2)
+        kv_sent(2)
+        send_shared(qs, qbuf, s_q, r_q)
+
+    def shared_here():
+        for i in range(NZ, NZ + 4):
+            landed(qbuf.at[pl.ds(i * half, half), :], r_q.at[i])
+
+    def part_of(f, c):
+        return functools.partial(f, c)
+
+    before = {0: part_of(together, 0), 2: part_of(together, 1), 4: shared_here, 6: part_of(together, 2), 9: part_of(together, 3)}
+    after = {
+        0: (start_shared,), 1: (part_of(farther, 1), part_of(ring_scene, 1)), 2: (part_of(near, 2),), 3: (part_of(own, 3),),
+        4: (part_of(farther, 2),), 5: (part_of(near, 3), part_of(ring_scene, 2),), 6: (part_of(farther, 3),), 7: (part_of(ring_scene, 3),), 8: (part_of(ring_scene, 4),),
+    }
 
     def step(t, unused):
-        c, i = t // 3, lax.rem(t, 3)
-
-        @pl.when(i == 0)
-        def _():
-            together(c)
-
+        late, odd = t // 6, lax.rem(t // 4, 2)
+        c = late * (t // 3) + (1 - late) * ((1 - odd) * (t // 2) + odd * (t - 4))
+        i = late * lax.rem(t, 3) + (1 - late) * ((1 - odd) * lax.rem(t, 2) + odd * 2)
+        for when, action in before.items():
+            pl.when(t == when)(action)
         rows = pl.ds(pl.multiple_of(i * count, 16), count)
         keys = pl.ds(pl.multiple_of(c * 2 * block, 16), 2 * block)
         at = (i // 2) * HD
         k_cols = pl.ds(pl.multiple_of(at, HD), HD)
         v_cols = pl.ds(pl.multiple_of(at + 2 * HD, HD), HD)
         attend(use_max, qbuf[rows, :], kv[keys, k_cols], kv[keys, v_cols], acc, best, rows)
-
-        @pl.when(jnp.logical_and(i == 0, c < 2))
-        def _():
-            own(c + 2)
-
-        @pl.when(jnp.logical_or(jnp.logical_and(i == 1, c < 2), t == 6))
-        def _():
-            farther(c + 1)
-
-        @pl.when(jnp.logical_and(i == 2, c < 2))
-        def _():
-            near(c + 2)
-
-        @pl.when(t == 3)
-        def _():
-            each_target(NEAREST, send_scene)
-
-        @pl.when(t == 6)
-        def _():
-            for k in range(NZ):
-                landed(scene.at[pl.ds(0, sc_half), :], r_s.at[k])
-            ref = scene_part(core, y)
-            for d in range(1, NY):
-                to = device(lax.rem(y + d, NY), z, core)
-                pltpu.make_async_remote_copy(ref, ref, s_sy.at[d - 1], r_sy.at[y], to, MESH).start()
-            share_scene(y)
+        for when, actions in after.items():
+
+            @pl.when(t == when)
+            def _():
+                for action in actions:
+                    action()
 
         for last in range(3):
 
@@ -354,10 +385,6 @@
         return unused
 
     lax.fori_loop(0, 12, step, 0)
-    for d in range(1, NY):
-        of_y = lax.rem(y + d, NY)
-        landed(scene_part(core, of_y), r_sy.at[of_y])
-        share_scene(of_y)
     landed(wo.at[my_rows, :], s_w.at[3])
     landed(wc, s_w.at[4])
     landed(wo.at[their_rows, :], r_x.at[1])
@@ -374,16 +401,20 @@
         whole = project(hid, wc, i)
         for at, h in ((0, 2 * i), (128, 2 * i + 1)):
             part = head_norm(whole[:, at : at + 128], cg_ref[...]).astype(BF16)
-            for j in range(4):
-                if MAIN[j] == h:
-                    cqm[j, :, :] = part
-                if SHARED[j] == h:
-                    cqs[j, :, :] = part
-    send_queries(cqm, cqs, cqbuf, s_cq, r_cq)
+            cq[h, :, :] = part
+
+    def send_cross_queries(i, g, u, to, same):
+        there = pl.ds(pl.multiple_of((i * NY + y) * half, 16), half)
+        src = cq.at[3 * g + i, pl.ds(u * half, half), :]
+        put(src, cqbuf.at[there, :], s_cq.at[i, g, u], r_cq.at[i, y], to, same)
+
+    for i in range(3):
+        each_ring(functools.partial(send_cross_queries, i))
     small = sc_out.at[0, pl.ds(0, sc_half), :]
-    kv_sent(2)
+    unit = cq.at[0, pl.ds(0, half), :]
     kv_sent(3)
-    each_target(NEAREST, lambda d, to_z, j, u, to, same: sent(small, s_s.at[d, u], same))
+    queries_sent((0, 4, 2, 6), s_q, 1)
+    each_ring(lambda g, u, to, same: sent(small, s_s.at[g, u], same))
     each_context((0, 1, 2), lambda i, src, to_z, head: sent(ctx.at[pl.ds(0, half), :], s_c.at[i], to_z == z))
     packet = kv_out.at[0, pl.ds(0, half), :]
     for slot in range(8):
@@ -392,23 +423,24 @@
         landed(packet, s_yp.at[1, slot] if slot % 2 == 0 else s_ym.at[1, slot])
         for of_y in range(NY):
             landed(packet, s_co.at[of_y, slot])
-    for i in range(NY):
+    for i in range(NZ):
         landed(scene_part(other, i), r_sc.at[i])
-        landed(scene_part(0, 0), s_sc.at[i])
+        landed(scene_part(core, i), s_sc.at[i])
+    for i in range(4):
+        landed(scene_part(core, 0), s_su.at[i])
         if i < 3:
-            landed(scene_part(0, 0), s_sy.at[i])
+            landed(scene_part(core, 0), s_sd.at[i])
     landed(mod.at[mine, :], s_x.at[0])
     landed(wo_ref, s_x.at[1])
     landed(hid.at[mine, :], s_x.at[2])
 
     def cross_step(i, unused):
-        for k in range(4):
-            unit = 4 * i + k
-            landed(cqbuf.at[pl.ds(pl.multiple_of(unit * half, 16), half), :], r_cq.at[unit])
+        for k in range(NY):
+            there = pl.ds(pl.multiple_of((i * NY + k) * half, 16), half)
+            landed(cqbuf.at[there, :], r_cq.at[i, k])
         rows = pl.ds(pl.multiple_of(i * count, 16), count)
-        at = (i // 2) * HD
-        k_cols = pl.ds(pl.multiple_of(at, HD), HD)
-        v_cols = pl.ds(pl.multiple_of(at + 2 * HD, HD), HD)
+        k_cols = pl.ds(pl.multiple_of(i * HD, HD), HD)
+        v_cols = pl.ds(pl.multiple_of((i + 3) * HD, HD), HD)
         s = scores_of(cqbuf[rows, :], scene[:, k_cols])
         p = jnp.exp2((s - jnp.max(s, axis=1, keepdims=True)) * SCALE2).astype(BF16)
         values = scene[:, v_cols]
@@ -419,7 +451,7 @@
 
             @pl.when(i == last)
             def _():
-                each_context((last,), send_cross)
+                each_cross(last, functools.partial(send_cross, last))
 
         return unused
 
@@ -427,13 +459,9 @@
     for head in range(6):
         for u in range(2):
             landed(out_ref.at[pl.ds(u * half, half), head * HD : (head + 1) * HD], r_cc.at[head, u])
-    queries_sent(s_cq)
-
-    def cross_sent(i, src, to_z, head):
-        same = jnp.logical_and(to_z == z, source_core(z) == core)
-        sent(ctx.at[pl.ds(0, half), :], s_cc.at[i], same)
-
-    each_context((0, 1, 2), cross_sent)
+    for i in range(3):
+        each_ring(lambda g, u, to, same: sent(unit, s_cq.at[i, g, u], same))
+        each_cross(i, lambda src, sem, to, same: sent(unit, sem, same))
 
 
 def whole_block(use_max, tokens, modulation, w_parts, w_out, w_cross, q_gain, k_gain, c_gain, sk, sv):
@@ -444,15 +472,15 @@
     sizes = [
         (w_parts.shape, BF16), ((2 * w_out.shape[0], width), BF16), (w_cross.shape, BF16), ((2 * half, width), BF16),
         ((4, 2 * half, 4 * HD), BF16), ((4, 2 * half, HD), BF16), ((4, 2 * half, HD), BF16),
-        ((4, 2 * sc_half, 4 * HD), BF16),
+        ((2, 2 * sc_half, 6 * HD), BF16),
         ((NY * NZ * 2 * half, 4 * HD), BF16), ((12 * half, HD), BF16),
         ((12 * half, 2 * HD), F32), ((12 * half, HD), F32), ((12 * half, HD), BF16), ((half, width), BF16),
-        ((2 * sc_half * NY * NZ, 4 * HD), BF16), ((2 * half, width), BF16),
-        ((4, 2 * half, HD), BF16), ((4, 2 * half, HD), BF16), ((12 * half, HD), BF16),
+        ((2 * sc_half * NY * NZ, 6 * HD), BF16), ((2 * half, width), BF16),
+        ((6, 2 * half, HD), BF16), ((12 * half, HD), BF16),
     ]
     sems = [
-        (5,), (3,), (3,), (8, 2), (8, 2), (8, 2, 2), (8, 2, 2), (2, 8), (2, 8), (4, 8), (3,), (4,), (12,), (12,),
-        (4, 8), (4, 8), (8,), (4,), (4,), (12,), (12,), (12,), (6, 2),
+        (5,), (3,), (3,), (8, 2), (2, 2), (8, 2, 2), (3, 2, 2), (2, 8), (2, 8), (4, 8), (4,), (3,), (8,), (12,), (12,),
+        (4, 8), (4, 8), (4,), (8,), (8,), (12,), (3, 4), (12,), (6, 2),
     ]
     return pl.pallas_call(
         functools.partial(block_kernel, use_max, half, sc_half),

time: 132 us -> 130 us (0.985)
    pallas_call x1, Pallas kernels: 126 us -> 125 us  [whole_block(): pl.pallas_call(functools.partial(block_kernel, use_max, half, sc_half), o...]
where the time goes in v3:
time: 130 us
  Pallas kernels  125 us (96%)
  other arithmetic  2 us (2%)
  local copies, waits for them, and re-layouts  1.53 us (1%)
    pallas_call x1, Pallas kernels, whole_block(): pl.pallas_call(functools.partial(block_kernel, use_max, half, sc_half), o...  125 us

profile of v3, /device:TPU:1, one launch (start us, length us, event | category | flops | bytes accessed | tf_op | source)
XLA Modules:
  0.0 129.9 jit_solution(6357080997440021493)
XLA Ops:
  0.6 0.7 abs.6
  1.3 0.7 abs.7
  1.9 0.7 multiply_reduce_fusion
  3.3 125.0 %conditional.1 = ((bf16[144,1536]{1,0:T(8,128)(2,1)S(1)}, bf16[288,768]{1,0:T(8,128)(2,1)S(1)})) conditional(s32[]{:T(128)} %convert_element_type.3, (bf16[144,1536]{1,0:T(8,128)(2,1)}, f32[3,1536]{1,0:T(4,128)}, bf16[3,1536,768]{2,1,0:T(8,128)(2,1)}, bf16[768,1536]{1,0:T(8,128)(2,1)}, bf16[1536,768]{1,0:T(8,128)(2,1)}, /*index=5*/f32[128]{0:T(128)}, ...), branch_computations={%region_1.0_spmd, %region_2.0_spmd} | conditional | bytes 8 | solution.py:504
  3.3 124.8 %branch_0_fun.1 = (bf16[144,1536]{1,0:T(8,128)(2,1)S(1)}, bf16[288,768]{1,0:T(8,128)(2,1)S(1)}) custom-call(bf16[144,1536]{1,0:T(8,128)(2,1)} %get-tuple-element.86.tok_ref, f32[3,1536]{1,0:T(4,128)} %get-tuple-element.88.mod_ref, bf16[3,1536,768]{2,1,0:T(8,128)(2,1)} %get-tuple-element.42.w_ref, bf16[768,1536]{1,0:T(8,128)(2,1)} %get-tuple-element.90.wo_ref, ...), custom_call_target="tpu_custom_call" | custom-call | tf_op jit(solution)/shard_map/cond/branch_0_fun/pallas_call | solution.py:485
  128.3 0.8 copy.36
  129.1 0.8 copy.37

commit v4 on v3

--- a/solution.py
+++ b/solution.py
@@ -352,7 +352,7 @@
     before = {0: part_of(together, 0), 2: part_of(together, 1), 4: shared_here, 6: part_of(together, 2), 9: part_of(together, 3)}
     after = {
         0: (start_shared,), 1: (part_of(farther, 1), part_of(ring_scene, 1)), 2: (part_of(near, 2),), 3: (part_of(own, 3),),
-        4: (part_of(farther, 2),), 5: (part_of(near, 3), part_of(ring_scene, 2),), 6: (part_of(farther, 3),), 7: (part_of(ring_scene, 3),), 8: (part_of(ring_scene, 4),),
+        4: (part_of(farther, 2),), 5: (part_of(near, 3), part_of(ring_scene, 2),), 6: (part_of(farther, 3),), 8: (part_of(ring_scene, 3),),
     }
 
     def step(t, unused):
@@ -385,6 +385,7 @@
         return unused
 
     lax.fori_loop(0, 12, step, 0)
+    ring_scene(4)
     landed(wo.at[my_rows, :], s_w.at[3])
     landed(wc, s_w.at[4])
     landed(wo.at[their_rows, :], r_x.at[1])

time: 130 us -> 129 us (level)
  no operation moved by 1% of the time
where the time goes in v4:
time: 129 us
  Pallas kernels  124 us (96%)
  other arithmetic  2 us (2%)
  local copies, waits for them, and re-layouts  1.53 us (1%)
  between operations  1.29 us (1%)
    pallas_call x1, Pallas kernels, whole_block(): pl.pallas_call(functools.partial(block_kernel, use_max, half, sc_half), o...  124 us

profile of v4, /device:TPU:1, one launch (start us, length us, event | category | flops | bytes accessed | tf_op | source)
XLA Modules:
  0.0 128.6 jit_solution(2205430414543892165)
XLA Ops:
  0.6 0.7 abs.6
  1.3 0.7 abs.7
  1.9 0.7 multiply_reduce_fusion
  3.3 123.8 %conditional.1 = ((bf16[144,1536]{1,0:T(8,128)(2,1)S(1)}, bf16[288,768]{1,0:T(8,128)(2,1)S(1)})) conditional(s32[]{:T(128)} %convert_element_type.3, (bf16[144,1536]{1,0:T(8,128)(2,1)}, f32[3,1536]{1,0:T(4,128)}, bf16[3,1536,768]{2,1,0:T(8,128)(2,1)}, bf16[768,1536]{1,0:T(8,128)(2,1)}, bf16[1536,768]{1,0:T(8,128)(2,1)}, /*index=5*/f32[128]{0:T(128)}, ...), branch_computations={%region_1.0_spmd, %region_2.0_spmd} | conditional | bytes 8 | solution.py:505
  3.3 123.5 %branch_0_fun.1 = (bf16[144,1536]{1,0:T(8,128)(2,1)S(1)}, bf16[288,768]{1,0:T(8,128)(2,1)S(1)}) custom-call(bf16[144,1536]{1,0:T(8,128)(2,1)} %get-tuple-element.86.tok_ref, f32[3,1536]{1,0:T(4,128)} %get-tuple-element.88.mod_ref, bf16[3,1536,768]{2,1,0:T(8,128)(2,1)} %get-tuple-element.42.w_ref, bf16[768,1536]{1,0:T(8,128)(2,1)} %get-tuple-element.90.wo_ref, ...), custom_call_target="tpu_custom_call" | custom-call | tf_op jit(solution)/shard_map/cond/branch_0_fun/pallas_call | solution.py:486
  127.0 0.8 copy.36
  127.8 0.8 copy.37
